TPU v7x, 32 devices: a whole 2x2x4 slice. The times are simulated.
32 devices in a mesh: segment: 4 (over y, core), dp: 2 (over x), expert: 4 (over z).
Axes of the slice: x: 2, y: 2, z: 4, core: 2. Of those that a mesh axis runs over, the one named last changes fastest.
Arguments:
- saved_b: bfloat16 [4, 1024, 2048], P('segment', ('dp', 'expert')), may hold values from -6 to 6
- route_b: int32 [4, 1024, 1], P('segment', ('dp', 'expert')), may hold values from 0 to 3; in each aligned block of 128 rows (0 to 127, 128 to 255, ..., all dimensions but the last counted through in order) at most 40 rows name the same one
- gate_b: float32 [4, 1024, 1], P('segment', ('dp', 'expert')), may hold values from 0.2 to 1
- grad_y_b: bfloat16 [4, 1024, 2048], P('segment', ('dp', 'expert')), may hold values from -6 to 6
- w_in: bfloat16 [4, 4, 2048, 768], P('segment', 'expert'), may hold values from -0.125 to 0.125
- w_out: bfloat16 [4, 4, 768, 2048], P('segment', 'expert'), may hold values from -0.21875 to 0.21875
Outputs:
- grad_x_b: bfloat16 [4, 1024, 2048], P('segment', ('dp', 'expert'))
- grad_in: bfloat16 [4, 4, 2048, 768], P('segment', 'expert', None, 'dp')
Inputs may be any that keep to these rules, and one draw needn't show every extreme that they name: `route_b`: of the 128 tokens of one device of a section, at most 40 pick any one expert; some device sends exactly 40 to some expert.
All inputs are finite; a program needn't handle non-finite values.
Results may differ from a plain program's by a relative error of at most 0.01.
Values may be sent and summed in bfloat16 or wider, within the bound.
A program may use at most 64 MiB of HBM per device.

v0:
```python
import jax
import jax.numpy as jnp
from jax import lax
from jax.sharding import PartitionSpec as P


def passed_along(value, axis, steps):
    count = lax.axis_size(axis)
    pairs = [(source, (source + steps) % count) for source in range(count)]
    return lax.ppermute(value, axis, pairs)


def silu_grad(value):
    sigma = jax.nn.sigmoid(value)
    return sigma * (1.0 + value * (1.0 - sigma))


def slot_table(expert_ids, capacity, experts):
    onehot = (expert_ids[:, None] == jnp.arange(experts, dtype=jnp.int32)[None, :]).astype(
        jnp.int32
    )
    before = jnp.cumsum(onehot, axis=0) - onehot
    position = expert_ids * capacity + jnp.sum(before * onehot, axis=1)
    slot_ids = jnp.arange(experts * capacity, dtype=jnp.int32)
    return (slot_ids[:, None] == position[None, :]).astype(jnp.bfloat16)


def dispatch(table, values, experts, capacity):
    placed = jnp.dot(table, values, preferred_element_type=jnp.float32).astype(jnp.bfloat16)
    return placed.reshape(experts, capacity, values.shape[1])


def combine(table, rows):
    return lax.dot_general(
        table, rows, (((0,), (0,)), ((), ())), preferred_element_type=jnp.float32
    )


def body(saved_b, route_b, gate_b, grad_y_b, w_in, w_out):
    experts = lax.axis_size("expert")
    tok_rows = saved_b.shape[1]
    model_width = saved_b.shape[2]
    capacity = max(2, tok_rows * 5 // (4 * experts))
    arrived = passed_along(grad_y_b, "segment", -1)[0]
    table_b = slot_table(route_b[0, :, 0], capacity, experts)
    scaled = (gate_b[0] * arrived.astype(jnp.float32)).astype(jnp.bfloat16)
    send_x = dispatch(table_b, saved_b[0], experts, capacity)
    send_g = dispatch(table_b, scaled, experts, capacity)
    recv_x, recv_g = (
        lax.all_to_all(send_x, "expert", split_axis=0, concat_axis=0, tiled=True),
        lax.all_to_all(send_g, "expert", split_axis=0, concat_axis=0, tiled=True),
    )
    rows_x = recv_x.reshape(-1, model_width)
    rows_g = recv_g.reshape(-1, model_width)
    weight_in = w_in[0, 0]
    weight_out = w_out[0, 0]
    pre_b = jnp.dot(rows_x, weight_in, preferred_element_type=jnp.float32)
    grad_h = lax.dot_general(
        rows_g, weight_out, (((1,), (1,)), ((), ())), preferred_element_type=jnp.float32
    )
    grad_pre = (grad_h * silu_grad(pre_b)).astype(jnp.bfloat16)
    grad_rows_x = lax.dot_general(
        grad_pre, weight_in, (((1,), (1,)), ((), ())), preferred_element_type=jnp.float32
    ).astype(jnp.bfloat16)
    back_x = lax.all_to_all(
        grad_rows_x.reshape(experts, capacity, model_width),
        "expert",
        split_axis=0,
        concat_axis=0,
        tiled=True,
    )
    grad_x = combine(table_b, back_x.reshape(-1, model_width)).astype(jnp.bfloat16)
    term_in = lax.dot_general(
        rows_x, grad_pre, (((0,), (0,)), ((), ())), preferred_element_type=jnp.float32
    )
    summed_in = lax.psum_scatter(
        term_in.astype(jnp.bfloat16), "dp", scatter_dimension=1, tiled=True
    )
    return (grad_x[None], summed_in[None, None])


def solution(mesh):
    return jax.shard_map(
        body,
        mesh=mesh,
        in_specs=(
            P("segment", ("dp", "expert"), None),
            P("segment", ("dp", "expert"), None),
            P("segment", ("dp", "expert"), None),
            P("segment", ("dp", "expert"), None),
            P("segment", "expert", None, None),
            P("segment", "expert", None, None),
        ),
        out_specs=(P("segment", ("dp", "expert"), None), P("segment", "expert", None, "dp")),
        check_vma=False,
    )
```

profile of v0, /device:TPU:0, one launch (start us, length us, event | category | flops | bytes accessed | tf_op | source)
XLA Modules:
  0.0 120.7 jit_solution(12892629107742777539)
XLA Ops:
  7.2 0.0 copy-start
  7.2 0.9 fusion.21
  8.1 0.2 reduce_window_sum.11
  8.2 0.8 select_reduce_fusion
  9.1 0.7 multiply_add_fusion
  9.7 2.2 %convolution_convert_fusion.1 = bf16[160,2048]{1,0:T(8,128)(2,1)} fusion(bf16[1,128,2048]{2,1,0:T(8,128)(2,1)} %param.6, s32[128]{0:T(128)S(1)} %multiply_add_fusion), kind=kOutput, calls=%fused_computation.8 | convolution fusion | flops 84234240 | bytes 1180160 | tf_op jit(solution)/shard_map/dot_general | solution.py:29
  12.0 6.3 %all-to-all-start.1 = ((bf16[4,40,2048]{2,1,0:T(8,128)(2,1)}), bf16[4,40,2048]{2,1,0:T(8,128)(2,1)}, u32[]{:S(2)}, u32[]{:S(2)}) async-start(bf16[4,40,2048]{2,1,0:T(8,128)(2,1)} %bitcast.44), calls=%async_computation.1 | async-start | bytes 1310720 | tf_op jit(solution)/shard_map/all_to_all | solution.py:50
  18.3 0.7 collective-permute-start
  19.0 7.0 %collective-permute-done = bf16[1,128,2048]{2,1,0:T(8,128)(2,1)S(1)} collective-permute-done((bf16[1,128,2048]{2,1,0:T(8,128)(2,1)}, bf16[1,128,2048]{2,1,0:T(8,128)(2,1)S(1)}, u32[]{:S(2)}, u32[]{:S(2)}) %collective-permute-start) | collective-permute-done | bytes 524320 | tf_op jit(solution)/shard_map/ppermute | solution.py:10
  26.0 1.9 %convolution_convert_fusion.2 = bf16[160,2048]{1,0:T(8,128)(2,1)} fusion(bf16[1,128,2048]{2,1,0:T(8,128)(2,1)S(1)} %collective-permute-done, f32[128]{0:T(128)} %bitcast.52, s32[128]{0:T(128)S(1)} %multiply_add_fusion), kind=kOutput, calls=%fused_computation.9 | convolution fusion | flops 85020672 | bytes 1180672 | tf_op jit(solution)/shard_map/dot_general | solution.py:29
  27.9 7.8 %all-to-all-done.1 = bf16[4,40,2048]{2,1,0:T(8,128)(2,1)} async-done(((bf16[4,40,2048]{2,1,0:T(8,128)(2,1)}), bf16[4,40,2048]{2,1,0:T(8,128)(2,1)}, u32[]{:S(2)}, u32[]{:S(2)}) %all-to-all-start.1) | async-done | bytes 655392 | tf_op jit(solution)/shard_map/all_to_all | solution.py:50
  35.7 4.2 %all-to-all-start = ((bf16[4,40,2048]{2,1,0:T(8,128)(2,1)}), bf16[4,40,2048]{2,1,0:T(8,128)(2,1)}, u32[]{:S(2)}, u32[]{:S(2)}) async-start(bf16[4,40,2048]{2,1,0:T(8,128)(2,1)} %bitcast.45), calls=%async_computation | async-start | bytes 1310720 | tf_op jit(solution)/shard_map/all_to_all | solution.py:51
  39.9 0.0 reduce-scatter.4.cloned.1.call-start
  39.9 0.0 copy-done
  39.9 2.5 %fusion.2 = f32[160,768]{1,0:T(8,128)} fusion(bf16[160,2048]{1,0:T(8,128)(2,1)} %bitcast.8, bf16[1,1,2048,768]{3,2,1,0:T(8,128)(2,1)S(1)} %copy-done), kind=kOutput, calls=%fused_computation.3 | convolution fusion | flops 503316480 | bytes 4292608 | tf_op jit(solution)/shard_map/dot_general | solution.py:57
  42.5 14.3 %all-to-all-done = bf16[4,40,2048]{2,1,0:T(8,128)(2,1)} async-done(((bf16[4,40,2048]{2,1,0:T(8,128)(2,1)}), bf16[4,40,2048]{2,1,0:T(8,128)(2,1)}, u32[]{:S(2)}, u32[]{:S(2)}) %all-to-all-start) | async-done | bytes 655392 | tf_op jit(solution)/shard_map/all_to_all | solution.py:51
  56.7 3.4 %fusion.13 = bf16[160,768]{1,0:T(8,128)(2,1)S(1)} fusion(bf16[160,2048]{1,0:T(8,128)(2,1)} %bitcast.4, bf16[1,1,768,2048]{3,2,1,0:T(8,128)(2,1)} %param.11, f32[160,768]{1,0:T(8,128)} %fusion.2), kind=kOutput, calls=%fused_computation.13 | convolution fusion | flops 504422400 | bytes 4538368 | tf_op jit(solution)/shard_map/dot_general | solution.py:58
  60.1 3.8 %convolution_convert_fusion = bf16[2048,768]{1,0:T(8,128)(2,1)} fusion(bf16[160,2048]{1,0:T(8,128)(2,1)} %bitcast.8, bf16[160,768]{1,0:T(8,128)(2,1)S(1)} %fusion.13), kind=kOutput, calls=%fused_computation | convolution fusion | flops 504889344 | bytes 4046848 | tf_op jit(solution)/shard_map/dot_general | solution.py:73
  63.9 4.7 %copy.8 = bf16[2048,768]{0,1:T(8,128)(2,1)} copy(bf16[2048,768]{1,0:T(8,128)(2,1)} %convolution_convert_fusion) | data formatting | bytes 6291456
  68.6 0.0 reduce-scatter.4.cloned.1.call-update
  68.6 1.2 fusion.6
  69.8 19.2 %all_to_all.15 = bf16[4,40,2048]{2,1,0:T(8,128)(2,1)S(1)} all-to-all(bf16[4,40,2048]{2,1,0:T(8,128)(2,1)S(1)} %bitcast.47), channel_id=1, replica_groups=mesh['segment'=4,'dp'=2,'expert'=4] {'expert'}, dimensions={0} | all-to-all | bytes 1310720 | tf_op jit(solution)/shard_map/all_to_all | solution.py:65
  89.0 1.1 fusion.9
  90.1 21.1 %reduce-scatter.4.cloned.1.call-done = bf16[384,2048]{1,0:T(8,128)(2,1)} async-done(((bf16[768,2048]{1,0:T(8,128)(2,1)}), bf16[384,2048]{1,0:T(8,128)(2,1)}) %reduce-scatter.4.cloned.1.call-update) | async-done | bytes 1572880
  111.2 2.6 %copy.9 = bf16[2048,384]{1,0:T(8,128)(2,1)} copy(bf16[2048,384]{0,1:T(8,128)(2,1)} %bitcast.48) | data formatting | bytes 3145728
Async XLA Ops:
  7.2 32.7 %copy-start = (bf16[1,1,2048,768]{3,2,1,0:T(8,128)(2,1)S(1)}, bf16[1,1,2048,768]{3,2,1,0:T(8,128)(2,1)}, u32[]{:S(2)}) copy-start(bf16[1,1,2048,768]{3,2,1,0:T(8,128)(2,1)} %param.10) | copy-start | bytes 9437188
  12.0 23.7 %all-to-all-start.1 = ((bf16[4,40,2048]{2,1,0:T(8,128)(2,1)}), bf16[4,40,2048]{2,1,0:T(8,128)(2,1)}, u32[]{:S(2)}, u32[]{:S(2)}) async-start(bf16[4,40,2048]{2,1,0:T(8,128)(2,1)} %bitcast.44), calls=%async_computation.1 | async-start | bytes 1310720 | tf_op jit(solution)/shard_map/all_to_all | solution.py:50
  18.3 7.7 %collective-permute-start = (bf16[1,128,2048]{2,1,0:T(8,128)(2,1)}, bf16[1,128,2048]{2,1,0:T(8,128)(2,1)S(1)}, u32[]{:S(2)}, u32[]{:S(2)}) collective-permute-start(bf16[1,128,2048]{2,1,0:T(8,128)(2,1)} %param.9), channel_id=1, source_target_pairs={{0,24},{8,0},{16,8},{24,16},{1,25},{9,1},{17,9},{25,17},{2,26},{10... | collective-permute-start | bytes 1572872 | tf_op jit(solution)/shard_map/ppermute | solution.py:10
  35.7 21.0 %all-to-all-start = ((bf16[4,40,2048]{2,1,0:T(8,128)(2,1)}), bf16[4,40,2048]{2,1,0:T(8,128)(2,1)}, u32[]{:S(2)}, u32[]{:S(2)}) async-start(bf16[4,40,2048]{2,1,0:T(8,128)(2,1)} %bitcast.45), calls=%async_computation | async-start | bytes 1310720 | tf_op jit(solution)/shard_map/all_to_all | solution.py:51
  39.9 71.4 %reduce-scatter.4.cloned.1.call-start = ((), (), s32[]{:S(2)}) async-start(), calls=%async_computation.4 | async-start | bytes 4718592
Sparse Core Ops, SparseCore 0:
  68.8 42.4 reduce-scatter.3
where the time goes:
time: 121 us
  waiting for transfers between devices  50.2 us (41%)
  blocking collectives  19.2 us (16%)
  matrix products  16.1 us (13%)
  between operations  14.1 us (12%)
  starting transfers between devices  11.2 us (9%)
  local copies, waits for them, and re-layouts  7.31 us (6%)
  other arithmetic  2.55 us (2%)
    unnamed x2, waiting for transfers between devices  21.1 us
    all_to_all x1, blocking collectives, body(): lax.all_to_all(grad_rows_x.reshape(experts, capacity, model_width), 'expe...  19.2 us
    all_to_all x1, waiting for transfers between devices, body(): lax.all_to_all(send_g, 'expert', split_axis=0, concat_axis=0, tiled=True)  14.3 us
    all_to_all x1, waiting for transfers between devices, body(): lax.all_to_all(send_x, 'expert', split_axis=0, concat_axis=0, tiled=True)  7.8 us
    unnamed x4, local copies, waits for them, and re-layouts  7.31 us
    ppermute x1, waiting for transfers between devices, passed_along(): return lax.ppermute(value, axis, pairs)  7.02 us
    all_to_all x1, starting transfers between devices, body(): lax.all_to_all(send_x, 'expert', split_axis=0, concat_axis=0, tiled=True)  6.32 us
    all_to_all x1, starting transfers between devices, body(): lax.all_to_all(send_g, 'expert', split_axis=0, concat_axis=0, tiled=True)  4.16 us
  transfers between devices with their start and end apart: 4, of which 4 were waited for; matrix products, arithmetic and copies ran while one was open for 6% of the time, Pallas kernels for 0%

commit v1 on v0

v1 whole, which is shorter than its diff:
```python
import functools
import jax
import jax.numpy as jnp
from jax import lax
from jax.experimental import pallas as pl
from jax.experimental.pallas import tpu as pltpu
from jax.sharding import PartitionSpec as P

F32 = jnp.float32
BF16 = jnp.bfloat16


def kernel(
    sizes,
    route_ref, gate_ref, saved_hbm, gy_hbm, win_hbm, wout_hbm,
    gx_hbm, gin_hbm,
    saved_v, cot, win_v, wout_v, send_x, send_g, x_all, g_all, dsilu,
    gp_send, gp_all, ret, back, acc, gx_v, gin_v,
    loc, seg_s, seg_r, xs, xr, gs, gr, fs, fr, ps, pr, bs, br, outs,
):
    n_seg, n_dp, n_exp, cap, chunks = sizes
    me_s, me_d, me_z = lax.axis_index("segment"), lax.axis_index("dp"), lax.axis_index("expert")
    tok, width = saved_v.shape
    hidden = win_v.shape[1]
    part = hidden // n_dp
    step = width // chunks

    def turn(i):
        return 1 + lax.rem(i + n_exp // 2 - 2, n_exp - 1)

    def to_of(i):
        return lax.rem(me_z + turn(i), n_exp)

    def from_of(i):
        return lax.rem(me_z + n_exp - turn(i), n_exp)

    def remote(src, dst, ss, rs, seg=None, dp=None, exp=None):
        dev = (
            me_s if seg is None else seg,
            me_d if dp is None else dp,
            me_z if exp is None else exp,
        )
        return pltpu.make_async_remote_copy(
            src_ref=src, dst_ref=dst, send_sem=ss, recv_sem=rs,
            device_id=dev, device_id_type=pl.DeviceIdType.MESH,
        )

    in_saved = pltpu.make_async_copy(saved_hbm.at[0], saved_v, loc.at[0])
    in_win = pltpu.make_async_copy(win_hbm.at[0, 0], win_v, loc.at[1])
    in_wout = pltpu.make_async_copy(wout_hbm.at[0, 0], wout_v, loc.at[2])
    in_saved.start()

    before_s = lax.rem(me_s + n_seg - 1, n_seg)
    after_s = lax.rem(me_s + 1, n_seg)
    barrier = pltpu.get_barrier_semaphore()
    peers = [(before_s, me_d, me_z), (after_s, me_d, me_z)]
    peers += [(me_s, lax.rem(me_d + d, n_dp), me_z) for d in range(1, n_dp)]
    peers += [(me_s, me_d, lax.rem(me_z + k, n_exp)) for k in range(1, n_exp)]
    for peer in peers:
        pl.semaphore_signal(barrier, inc=1, device_id=peer, device_id_type=pl.DeviceIdType.MESH)

    rows_t = lax.broadcasted_iota(jnp.int32, (tok, tok), 0)
    cols_t = lax.broadcasted_iota(jnp.int32, (tok, tok), 1)
    route = jnp.sum(jnp.where(rows_t == cols_t, route_ref[...], 0), axis=1, keepdims=True)
    gate = jnp.sum(jnp.where(rows_t == cols_t, gate_ref[...], 0.0), axis=1, keepdims=True)
    lanes = lax.broadcasted_iota(jnp.int32, (tok, 128), 1)
    onehot = (route == lanes).astype(F32)
    lower = (cols_t < rows_t).astype(BF16)
    ahead = jnp.dot(lower, onehot.astype(BF16), preferred_element_type=F32)
    rank = jnp.sum(ahead * onehot, axis=1, keepdims=True).astype(jnp.int32)
    pos_col = route * cap + rank
    pos_row = jnp.sum(jnp.where(rows_t == cols_t, pos_col, 0), axis=0, keepdims=True)

    def table(expert):
        slots = lax.broadcasted_iota(jnp.int32, (cap, tok), 0) + expert * cap
        return (slots == pos_row).astype(F32).astype(BF16)

    def table_t(expert):
        slots = lax.broadcasted_iota(jnp.int32, (tok, cap), 1) + expert * cap
        return (slots == pos_col).astype(F32).astype(BF16)

    pl.semaphore_wait(barrier, len(peers))
    seg_copy = remote(gy_hbm.at[0], cot, seg_s.at[0], seg_r.at[0], seg=before_s)
    seg_copy.start()
    in_saved.wait()
    saved = saved_v[...]

    def x_copy(i):
        return remote(send_x.at[i - 1], x_all.at[me_d, me_z], xs.at[i - 1], xr.at[me_z], exp=to_of(i))

    for i in range(1, n_exp):
        send_x[i - 1] = jnp.dot(table(to_of(i)), saved, preferred_element_type=F32).astype(BF16)
        x_copy(i).start()
    in_win.start()
    in_wout.start()
    x_all[me_d, me_z] = jnp.dot(table(me_z), saved, preferred_element_type=F32).astype(BF16)

    def forward(d, block):
        return remote(
            x_all.at[me_d, block], x_all.at[me_d, block],
            fs.at[d - 1, block], fr.at[me_d, block], dp=lax.rem(me_d + d, n_dp),
        )

    for d in range(1, n_dp):
        forward(d, me_z).start()

    seg_copy.wait_recv()
    scaled = (gate * cot[...].astype(F32)).astype(BF16)

    def g_copy(i):
        return remote(send_g.at[i - 1], g_all.at[me_z], gs.at[i - 1], gr.at[me_z], exp=to_of(i))

    for i in range(1, n_exp):
        send_g[i - 1] = jnp.dot(table(to_of(i)), scaled, preferred_element_type=F32).astype(BF16)
        g_copy(i).start()
    g_all[me_z] = jnp.dot(table(me_z), scaled, preferred_element_type=F32).astype(BF16)

    for i in range(1, n_exp):
        block = from_of(i)
        remote(send_x.at[i - 1], x_all.at[me_d, block], xs.at[i - 1], xr.at[block], exp=block).wait_recv()
        for d in range(1, n_dp):
            forward(d, block).start()

    in_win.wait()
    own_x = x_all[me_d].astype(F32).reshape(n_exp * cap, width).astype(BF16)
    pre = jnp.dot(own_x, win_v[...], preferred_element_type=F32)
    sigma = jax.nn.sigmoid(pre)
    dsilu[...] = (sigma * (1.0 + pre * (1.0 - sigma))).reshape(n_exp, cap, hidden)
    in_wout.wait()

    def expert_block(block):
        grad_h = lax.dot_general(
            g_all[block], wout_v[...], (((1,), (1,)), ((), ())), preferred_element_type=F32
        )
        grad_pre = (grad_h * dsilu[block]).astype(BF16)
        for j in range(n_dp):
            gp_send[j, block] = grad_pre[:, j * part:(j + 1) * part]
        return lax.dot_general(
            grad_pre, win_v[...], (((1,), (1,)), ((), ())), preferred_element_type=F32
        ).astype(BF16)

    def b_copy(i, block):
        return remote(ret.at[i - 1], back.at[me_z], bs.at[i - 1], br.at[me_z], exp=block)

    back[me_z] = expert_block(me_z)

    def one_block(i, carry):
        block = from_of(i)
        remote(send_g.at[i - 1], g_all.at[block], gs.at[i - 1], gr.at[block], exp=block).wait_recv()
        ret[i - 1] = expert_block(block)
        b_copy(i, block).start()
        return carry

    lax.fori_loop(1, n_exp, one_block, 0)

    def p_copy(d):
        other = lax.rem(me_d + d, n_dp)
        return remote(gp_send.at[other], gp_all.at[me_d], ps.at[d - 1], pr.at[me_d], dp=other)

    for d in range(1, n_dp):
        p_copy(d).start()
    gp_all[me_d] = gp_send[me_d]
    acc[...] = jnp.dot(table_t(me_z), back[me_z], preferred_element_type=F32)

    for d in range(1, n_dp):
        other = lax.rem(me_d + n_dp - d, n_dp)
        for block in range(n_exp):
            remote(
                x_all.at[other, block], x_all.at[other, block],
                fs.at[d - 1, block], fr.at[other, block], dp=other,
            ).wait_recv()
        remote(gp_send.at[other], gp_all.at[other], ps.at[d - 1], pr.at[other], dp=other).wait_recv()

    all_gp = gp_all[...].astype(F32).reshape(n_dp * n_exp * cap, part).astype(BF16)

    def out_copy(c):
        rows = pl.ds(pl.multiple_of(c * step, step), step)
        return pltpu.make_async_copy(gin_v.at[rows], gin_hbm.at[rows], outs.at[c])

    def one_chunk(c, carry):
        at = pl.ds(pl.multiple_of(c * step, step), step)
        xs_c = x_all[:, :, :, at].astype(F32).reshape(n_dp * n_exp * cap, step).astype(BF16)
        gin_v[at, :] = lax.dot_general(
            xs_c, all_gp, (((0,), (0,)), ((), ())), preferred_element_type=F32
        ).astype(BF16)
        out_copy(c).start()
        return carry

    lax.fori_loop(0, chunks, one_chunk, 0)

    for i in range(1, n_exp):
        block = from_of(i)
        remote(ret.at[i - 1], back.at[block], bs.at[i - 1], br.at[block], exp=block).wait_recv()
        acc[...] += jnp.dot(table_t(block), back[block], preferred_element_type=F32)
    gx_v[...] = acc[...].astype(BF16)
    out_x = pltpu.make_async_copy(gx_v, gx_hbm, loc.at[3])
    out_x.start()

    seg_copy.wait_send()
    for i in range(1, n_exp):
        x_copy(i).wait_send()
        g_copy(i).wait_send()
        b_copy(i, from_of(i)).wait_send()
    for d in range(1, n_dp):
        for block in range(n_exp):
            forward(d, block).wait_send()
        p_copy(d).wait_send()
    for c in range(chunks):
        out_copy(c).wait()
    out_x.wait()


def body(saved_b, route_b, gate_b, grad_y_b, w_in, w_out):
    n_seg, n_dp, n_exp = lax.axis_size("segment"), lax.axis_size("dp"), lax.axis_size("expert")
    tok, width = saved_b.shape[1], saved_b.shape[2]
    hidden = w_in.shape[3]
    part = hidden // n_dp
    most = max(2, tok * 5 // (4 * n_exp))
    cap = -(-most // 8) * 8
    chunks = 4
    vmem = pl.BlockSpec(memory_space=pltpu.VMEM)
    hbm = pl.BlockSpec(memory_space=pl.ANY)
    dma = pltpu.SemaphoreType.DMA
    flops = 8 * n_exp * cap * width * hidden
    grad_x, grad_in = pl.pallas_call(
        functools.partial(kernel, (n_seg, n_dp, n_exp, cap, chunks)),
        out_shape=(
            jax.ShapeDtypeStruct((tok, width), BF16),
            jax.ShapeDtypeStruct((width, part), BF16),
        ),
        in_specs=[vmem, vmem, hbm, hbm, hbm, hbm],
        out_specs=(hbm, hbm),
        scratch_shapes=[
            pltpu.VMEM((tok, width), BF16),
            pltpu.VMEM((tok, width), BF16),
            pltpu.VMEM((width, hidden), BF16),
            pltpu.VMEM((hidden, width), BF16),
            pltpu.VMEM((n_exp - 1, cap, width), BF16),
            pltpu.VMEM((n_exp - 1, cap, width), BF16),
            pltpu.VMEM((n_dp, n_exp, cap, width), BF16),
            pltpu.VMEM((n_exp, cap, width), BF16),
            pltpu.VMEM((n_exp, cap, hidden), F32),
            pltpu.VMEM((n_dp, n_exp, cap, part), BF16),
            pltpu.VMEM((n_dp, n_exp, cap, part), BF16),
            pltpu.VMEM((n_exp - 1, cap, width), BF16),
            pltpu.VMEM((n_exp, cap, width), BF16),
            pltpu.VMEM((tok, width), F32),
            pltpu.VMEM((tok, width), BF16),
            pltpu.VMEM((width, part), BF16),
            dma((4,)),
            dma((1,)), dma((1,)),
            dma((n_exp,)), dma((n_exp,)),
            dma((n_exp,)), dma((n_exp,)),
            dma((n_dp, n_exp)), dma((n_dp, n_exp)),
            dma((n_dp,)), dma((n_dp,)),
            dma((n_exp,)), dma((n_exp,)),
            dma((chunks,)),
        ],
        compiler_params=pltpu.CompilerParams(
            collective_id=0, has_side_effects=True, vmem_limit_bytes=56 * 1024 * 1024
        ),
        cost_estimate=pl.CostEstimate(flops=flops, bytes_accessed=10 * 1024 * 1024, transcendentals=0),
    )(route_b.reshape(1, tok), gate_b.reshape(1, tok), saved_b, grad_y_b, w_in, w_out)
    return (grad_x[None], grad_in[None, None])


def solution(mesh):
    return jax.shard_map(
        body,
        mesh=mesh,
        in_specs=(
            P("segment", ("dp", "expert"), None),
            P("segment", ("dp", "expert"), None),
            P("segment", ("dp", "expert"), None),
            P("segment", ("dp", "expert"), None),
            P("segment", "expert", None, None),
            P("segment", "expert", None, None),
        ),
        out_specs=(P("segment", ("dp", "expert"), None), P("segment", "expert", None, "dp")),
        check_vma=False,
    )
```

time: 121 us -> 56.2 us (0.46)
  Pallas kernels: 0 us -> 50.8 us
  waiting for transfers between devices: 50.2 us -> 0 us
  blocking collectives: 19.2 us -> 0 us
  matrix products: 16.1 us -> 0 us
  between operations: 14.1 us -> 0.64 us
  starting transfers between devices: 11.2 us -> 0 us
  local copies, waits for them, and re-layouts: 7.31 us -> 4.59 us
  other arithmetic: 2.55 us -> 0 us
    pallas_call x0 -> x1, Pallas kernels: none -> 50.8 us  [body(): pl.pallas_call(functools.partial(kernel, (n_seg, n_dp, n_exp, cap, chunks...]
    all_to_all x2 -> x0, waiting for transfers between devices: 22.1 us -> none  [the longest x1 14.3 us: body(): lax.all_to_all(send_g, 'expert', split_axis=0, concat_axis=0, tiled=True)]
    unnamed x2 -> x0, waiting for transfers between devices: 21.1 us -> none
    all_to_all x1 -> x0, blocking collectives: 19.2 us -> none  [body(): lax.all_to_all(grad_rows_x.reshape(experts, capacity, model_width), 'expe...]
    dot_general x7 -> x0, matrix products: 16.1 us -> none  [the longest x2 4.12 us: dispatch(): jnp.dot(table, values, preferred_element_type=jnp.float32)]
    all_to_all x2 -> x0, starting transfers between devices: 10.5 us -> none  [the longest x1 6.32 us: body(): lax.all_to_all(send_x, 'expert', split_axis=0, concat_axis=0, tiled=True)]
    ppermute x1 -> x0, waiting for transfers between devices: 7.02 us -> none  [passed_along(): return lax.ppermute(value, axis, pairs)]
    unnamed x4 -> x2, local copies, waits for them, and re-layouts: 7.31 us -> 4.59 us
  transfers between devices with their start and end apart: 4 -> 0, of which waited for: 4 -> 0; matrix products, arithmetic and copies ran while one was open for 6% -> 0% of each run, Pallas kernels for 0% -> 0%
where the time goes in v1:
time: 56.2 us; the launch traced here: 56 us
  Pallas kernels  50.8 us (90%)
  local copies, waits for them, and re-layouts  4.59 us (8%)
  between operations  0.64 us (1%)
    pallas_call x1, Pallas kernels, body(): pl.pallas_call(functools.partial(kernel, (n_seg, n_dp, n_exp, cap, chunks...  50.8 us
    unnamed x2, local copies, waits for them, and re-layouts  4.59 us

profile of v1, /device:TPU:0, one launch (start us, length us, event | category | flops | bytes accessed | tf_op | source)
XLA Modules:
  0.0 56.0 jit_solution(11007865787346271799)
XLA Ops:
  0.6 50.8 %shard_map.77 = (bf16[128,2048]{1,0:T(8,128)(2,1)}, bf16[2048,384]{1,0:T(8,128)(2,1)}) custom-call(s32[1,128]{1,0:T(1,128)} %bitcast.6, f32[1,128]{1,0:T(1,128)} %bitcast.7, bf16[1,128,2048]{2,1,0:T(8,128)(2,1)} %saved_hbm.1, bf16[1,128,2048]{2,1,0:T(8,128)(2,1)} %gy_hbm.1, bf16[1,1,2048,768]{3,2,1,0:T(8,128)(2,1)} %win_hbm.1, bf16[1,1,768,2048]{3,2,1,0:T(8,128)(2,1)} %wout_hbm.1), custom_call_target="tpu_custom_call" | custom-call | flops 2013265920 | bytes 10485760 | tf_op jit(solution)/shard_map/pallas_call | solution.py:225
  51.4 1.9 %copy.10 = bf16[1,128,2048]{2,1,0:T(8,128)(2,1)} copy(bf16[1,128,2048]{2,1,0:T(8,128)(2,1)} %bitcast.5) | data formatting | bytes 1048576
  53.3 2.7 %copy.11 = bf16[1,1,2048,384]{3,2,1,0:T(8,128)(2,1)} copy(bf16[1,1,2048,384]{3,2,1,0:T(8,128)(2,1)} %bitcast.4) | data formatting | bytes 3145728

commit v2 on v1

--- a/solution.py
+++ b/solution.py
@@ -25,14 +25,23 @@
     part = hidden // n_dp
     step = width // chunks
 
-    def turn(i):
-        return 1 + lax.rem(i + n_exp // 2 - 2, n_exp - 1)
-
-    def to_of(i):
-        return lax.rem(me_z + turn(i), n_exp)
-
-    def from_of(i):
-        return lax.rem(me_z + n_exp - turn(i), n_exp)
+    paired = n_exp & (n_exp - 1) == 0
+
+    def flip(k):
+        other, bit = me_z, 1
+        while bit < n_exp:
+            other = other + bit * (k // bit % 2) * (1 - 2 * (me_z // bit % 2))
+            bit *= 2
+        return other
+
+    def to_of(k):
+        return flip(k) if paired else lax.rem(me_z + k, n_exp)
+
+    def from_of(k):
+        return flip(k) if paired else lax.rem(me_z + n_exp - k, n_exp)
+
+    near_first = list(range(1, n_exp))
+    far_first = near_first[n_exp // 2 - 1:] + near_first[:n_exp // 2 - 1]
 
     def remote(src, dst, ss, rs, seg=None, dp=None, exp=None):
         dev = (
@@ -88,7 +97,7 @@
     def x_copy(i):
         return remote(send_x.at[i - 1], x_all.at[me_d, me_z], xs.at[i - 1], xr.at[me_z], exp=to_of(i))
 
-    for i in range(1, n_exp):
+    for i in far_first:
         send_x[i - 1] = jnp.dot(table(to_of(i)), saved, preferred_element_type=F32).astype(BF16)
         x_copy(i).start()
     in_win.start()
@@ -191,8 +200,11 @@
     for i in range(1, n_exp):
         block = from_of(i)
         remote(ret.at[i - 1], back.at[block], bs.at[i - 1], br.at[block], exp=block).wait_recv()
-        acc[...] += jnp.dot(table_t(block), back[block], preferred_element_type=F32)
-    gx_v[...] = acc[...].astype(BF16)
+        total = acc[...] + jnp.dot(table_t(block), back[block], preferred_element_type=F32)
+        if i < n_exp - 1:
+            acc[...] = total
+        else:
+            gx_v[...] = total.astype(BF16)
     out_x = pltpu.make_async_copy(gx_v, gx_hbm, loc.at[3])
     out_x.start()
 
@@ -208,6 +220,19 @@
     for c in range(chunks):
         out_copy(c).wait()
     out_x.wait()
+
+
+def hand_on(pieces, gx_ref, gin_ref, gx_out, gin_out, sems):
+    copies = []
+    for src, dst in ((gin_ref, gin_out), (gx_ref, gx_out)):
+        rows = src.shape[0] // pieces
+        for p in range(pieces):
+            at = pl.ds(p * rows, rows)
+            copies.append(pltpu.make_async_copy(src.at[at], dst.at[at], sems.at[len(copies)]))
+    for copy in copies:
+        copy.start()
+    for copy in copies:
+        copy.wait()
 
 
 def body(saved_b, route_b, gate_b, grad_y_b, w_in, w_out):
@@ -261,6 +286,18 @@
         ),
         cost_estimate=pl.CostEstimate(flops=flops, bytes_accessed=10 * 1024 * 1024, transcendentals=0),
     )(route_b.reshape(1, tok), gate_b.reshape(1, tok), saved_b, grad_y_b, w_in, w_out)
+    pieces = 4
+    grad_x, grad_in = pl.pallas_call(
+        functools.partial(hand_on, pieces),
+        out_shape=(
+            jax.ShapeDtypeStruct((tok, width), BF16),
+            jax.ShapeDtypeStruct((width, part), BF16),
+        ),
+        in_specs=[hbm, hbm],
+        out_specs=(hbm, hbm),
+        scratch_shapes=[dma((2 * pieces,))],
+        compiler_params=pltpu.CompilerParams(vmem_limit_bytes=56 * 1024 * 1024),
+    )(grad_x, grad_in)
     return (grad_x[None], grad_in[None, None])
 
 

time: 56.2 us -> 116 us (2.06); the launches traced: 56 us -> 114 us
  Pallas kernels: 50.8 us -> 114 us
  local copies, waits for them, and re-layouts: 4.59 us -> 0 us
    pallas_call x0 -> x1, Pallas kernels: none -> 64.7 us  [body(): pl.pallas_call(functools.partial(hand_on, pieces), out_shape=(jax.ShapeDt...]
    unnamed x2 -> x0, local copies, waits for them, and re-layouts: 4.59 us -> none
    pallas_call x1, Pallas kernels: 50.8 us -> 48.9 us  [body(): pl.pallas_call(functools.partial(kernel, (n_seg, n_dp, n_exp, cap, chunks...]
where the time goes in v2:
time: 116 us; the launch traced here: 114 us
  Pallas kernels  114 us (98%)
    pallas_call x1, Pallas kernels, body(): pl.pallas_call(functools.partial(hand_on, pieces), out_shape=(jax.ShapeDt...  64.7 us
    pallas_call x1, Pallas kernels, body(): pl.pallas_call(functools.partial(kernel, (n_seg, n_dp, n_exp, cap, chunks...  48.9 us

profile of v2, /device:TPU:0, one launch (start us, length us, event | category | flops | bytes accessed | tf_op | source)
XLA Modules:
  0.0 114.2 jit_solution(5833046115794770276)
XLA Ops:
  0.6 48.9 %shard_map.77 = (bf16[128,2048]{1,0:T(8,128)(2,1)}, bf16[2048,384]{1,0:T(8,128)(2,1)}) custom-call(s32[1,128]{1,0:T(1,128)} %bitcast.6, f32[1,128]{1,0:T(1,128)} %bitcast.7, bf16[1,128,2048]{2,1,0:T(8,128)(2,1)} %saved_hbm.1, bf16[1,128,2048]{2,1,0:T(8,128)(2,1)} %gy_hbm.1, bf16[1,1,2048,768]{3,2,1,0:T(8,128)(2,1)} %win_hbm.1, bf16[1,1,768,2048]{3,2,1,0:T(8,128)(2,1)} %wout_hbm.1), custom_call_target="tpu_custom_call" | custom-call | flops 2013265920 | bytes 10485760 | tf_op jit(solution)/shard_map/pallas_call | solution.py:250
  49.5 64.7 %shard_map.78 = (bf16[128,2048]{1,0:T(8,128)(2,1)}, bf16[2048,384]{1,0:T(8,128)(2,1)}) custom-call(bf16[128,2048]{1,0:T(8,128)(2,1)} %get-tuple-element.6.gx_ref, bf16[2048,384]{1,0:T(8,128)(2,1)} %get-tuple-element.7.gin_ref), custom_call_target="tpu_custom_call" | custom-call | tf_op jit(solution)/shard_map/pallas_call | solution.py:290

commit v3 on v2

--- a/solution.py
+++ b/solution.py
@@ -40,8 +40,11 @@
     def from_of(k):
         return flip(k) if paired else lax.rem(me_z + n_exp - k, n_exp)
 
-    near_first = list(range(1, n_exp))
-    far_first = near_first[n_exp // 2 - 1:] + near_first[:n_exp // 2 - 1]
+    half = max(1, n_exp // 2)
+    inner = (me_z + half // 2) // half % 2
+
+    def order(i, far_first):
+        return 1 + lax.rem(i - 1 + far_first * (half - 1), max(1, n_exp - 1))
 
     def remote(src, dst, ss, rs, seg=None, dp=None, exp=None):
         dev = (
@@ -97,9 +100,10 @@
     def x_copy(i):
         return remote(send_x.at[i - 1], x_all.at[me_d, me_z], xs.at[i - 1], xr.at[me_z], exp=to_of(i))
 
-    for i in far_first:
-        send_x[i - 1] = jnp.dot(table(to_of(i)), saved, preferred_element_type=F32).astype(BF16)
-        x_copy(i).start()
+    for i in range(1, n_exp):
+        k = order(i, inner)
+        send_x[k - 1] = jnp.dot(table(to_of(k)), saved, preferred_element_type=F32).astype(BF16)
+        x_copy(k).start()
     in_win.start()
     in_wout.start()
     x_all[me_d, me_z] = jnp.dot(table(me_z), saved, preferred_element_type=F32).astype(BF16)
@@ -120,13 +124,15 @@
         return remote(send_g.at[i - 1], g_all.at[me_z], gs.at[i - 1], gr.at[me_z], exp=to_of(i))
 
     for i in range(1, n_exp):
-        send_g[i - 1] = jnp.dot(table(to_of(i)), scaled, preferred_element_type=F32).astype(BF16)
-        g_copy(i).start()
+        k = order(i, inner)
+        send_g[k - 1] = jnp.dot(table(to_of(k)), scaled, preferred_element_type=F32).astype(BF16)
+        g_copy(k).start()
     g_all[me_z] = jnp.dot(table(me_z), scaled, preferred_element_type=F32).astype(BF16)
 
     for i in range(1, n_exp):
-        block = from_of(i)
-        remote(send_x.at[i - 1], x_all.at[me_d, block], xs.at[i - 1], xr.at[block], exp=block).wait_recv()
+        k = order(i, 1 - inner)
+        block = from_of(k)
+        remote(send_x.at[k - 1], x_all.at[me_d, block], xs.at[k - 1], xr.at[block], exp=block).wait_recv()
         for d in range(1, n_dp):
             forward(d, block).start()
 
@@ -154,10 +160,11 @@
     back[me_z] = expert_block(me_z)
 
     def one_block(i, carry):
-        block = from_of(i)
-        remote(send_g.at[i - 1], g_all.at[block], gs.at[i - 1], gr.at[block], exp=block).wait_recv()
-        ret[i - 1] = expert_block(block)
-        b_copy(i, block).start()
+        k = order(i, 1 - inner)
+        block = from_of(k)
+        remote(send_g.at[k - 1], g_all.at[block], gs.at[k - 1], gr.at[block], exp=block).wait_recv()
+        ret[k - 1] = expert_block(block)
+        b_copy(k, block).start()
         return carry
 
     lax.fori_loop(1, n_exp, one_block, 0)
@@ -198,8 +205,9 @@
     lax.fori_loop(0, chunks, one_chunk, 0)
 
     for i in range(1, n_exp):
-        block = from_of(i)
-        remote(ret.at[i - 1], back.at[block], bs.at[i - 1], br.at[block], exp=block).wait_recv()
+        k = order(i, inner)
+        block = to_of(k)
+        remote(ret.at[k - 1], back.at[block], bs.at[k - 1], br.at[block], exp=block).wait_recv()
         total = acc[...] + jnp.dot(table_t(block), back[block], preferred_element_type=F32)
         if i < n_exp - 1:
             acc[...] = total
@@ -222,17 +230,21 @@
     out_x.wait()
 
 
-def hand_on(pieces, gx_ref, gin_ref, gx_out, gin_out, sems):
-    copies = []
-    for src, dst in ((gin_ref, gin_out), (gx_ref, gx_out)):
+def hand_on(pieces, gx_ref, gin_ref, gx_out, gin_out, gx_v, gin_v, sems):
+    loads, stores = [], []
+    for src, mid, dst in ((gin_ref, gin_v, gin_out), (gx_ref, gx_v, gx_out)):
         rows = src.shape[0] // pieces
         for p in range(pieces):
             at = pl.ds(p * rows, rows)
-            copies.append(pltpu.make_async_copy(src.at[at], dst.at[at], sems.at[len(copies)]))
-    for copy in copies:
-        copy.start()
-    for copy in copies:
-        copy.wait()
+            loads.append(pltpu.make_async_copy(src.at[at], mid.at[at], sems.at[0, len(loads)]))
+            stores.append(pltpu.make_async_copy(mid.at[at], dst.at[at], sems.at[1, len(stores)]))
+    for load in loads:
+        load.start()
+    for load, store in zip(loads, stores):
+        load.wait()
+        store.start()
+    for store in stores:
+        store.wait()
 
 
 def body(saved_b, route_b, gate_b, grad_y_b, w_in, w_out):
@@ -295,7 +307,9 @@
         ),
         in_specs=[hbm, hbm],
         out_specs=(hbm, hbm),
-        scratch_shapes=[dma((2 * pieces,))],
+        scratch_shapes=[
+            pltpu.VMEM((tok, width), BF16), pltpu.VMEM((width, part), BF16), dma((2, 2 * pieces)),
+        ],
         compiler_params=pltpu.CompilerParams(vmem_limit_bytes=56 * 1024 * 1024),
     )(grad_x, grad_in)
     return (grad_x[None], grad_in[None, None])

time: 116 us -> 52.9 us (0.46)
  Pallas kernels: 114 us -> 51.3 us
    pallas_call x1, Pallas kernels: 64.7 us -> 2.44 us  [body(): pl.pallas_call(functools.partial(hand_on, pieces), out_shape=(jax.ShapeDt...]
where the time goes in v3:
time: 52.9 us; the launch traced here: 51.9 us
  Pallas kernels  51.3 us (97%)
  between operations  0.64 us (1%)
    pallas_call x1, Pallas kernels, body(): pl.pallas_call(functools.partial(kernel, (n_seg, n_dp, n_exp, cap, chunks...  48.8 us
    pallas_call x1, Pallas kernels, body(): pl.pallas_call(functools.partial(hand_on, pieces), out_shape=(jax.ShapeDt...  2.44 us

profile of v3, /device:TPU:0, one launch (start us, length us, event | category | flops | bytes accessed | tf_op | source)
XLA Modules:
  0.0 51.9 jit_solution(5745728774057080135)
XLA Ops:
  0.6 48.8 %shard_map.77 = (bf16[128,2048]{1,0:T(8,128)(2,1)}, bf16[2048,384]{1,0:T(8,128)(2,1)}) custom-call(s32[1,128]{1,0:T(1,128)} %bitcast.6, f32[1,128]{1,0:T(1,128)} %bitcast.7, bf16[1,128,2048]{2,1,0:T(8,128)(2,1)} %saved_hbm.1, bf16[1,128,2048]{2,1,0:T(8,128)(2,1)} %gy_hbm.1, bf16[1,1,2048,768]{3,2,1,0:T(8,128)(2,1)} %win_hbm.1, bf16[1,1,768,2048]{3,2,1,0:T(8,128)(2,1)} %wout_hbm.1), custom_call_target="tpu_custom_call" | custom-call | flops 2013265920 | bytes 10485760 | tf_op jit(solution)/shard_map/pallas_call | solution.py:262
  49.5 2.4 %shard_map.78 = (bf16[128,2048]{1,0:T(8,128)(2,1)}, bf16[2048,384]{1,0:T(8,128)(2,1)}) custom-call(bf16[128,2048]{1,0:T(8,128)(2,1)} %get-tuple-element.6.gx_ref, bf16[2048,384]{1,0:T(8,128)(2,1)} %get-tuple-element.7.gin_ref), custom_call_target="tpu_custom_call" | custom-call | tf_op jit(solution)/shard_map/pallas_call | solution.py:302

commit v4 on v3

--- a/solution.py
+++ b/solution.py
@@ -98,7 +98,7 @@
     saved = saved_v[...]
 
     def x_copy(i):
-        return remote(send_x.at[i - 1], x_all.at[me_d, me_z], xs.at[i - 1], xr.at[me_z], exp=to_of(i))
+        return remote(send_x.at[i - 1], x_all.at[me_d, i], xs.at[i - 1], xr.at[i], exp=to_of(i))
 
     for i in range(1, n_exp):
         k = order(i, inner)
@@ -106,7 +106,7 @@
         x_copy(k).start()
     in_win.start()
     in_wout.start()
-    x_all[me_d, me_z] = jnp.dot(table(me_z), saved, preferred_element_type=F32).astype(BF16)
+    x_all[me_d, 0] = jnp.dot(table(me_z), saved, preferred_element_type=F32).astype(BF16)
 
     def forward(d, block):
         return remote(
@@ -115,26 +115,25 @@
         )
 
     for d in range(1, n_dp):
-        forward(d, me_z).start()
+        forward(d, 0).start()
 
     seg_copy.wait_recv()
     scaled = (gate * cot[...].astype(F32)).astype(BF16)
 
     def g_copy(i):
-        return remote(send_g.at[i - 1], g_all.at[me_z], gs.at[i - 1], gr.at[me_z], exp=to_of(i))
+        return remote(send_g.at[i - 1], g_all.at[i], gs.at[i - 1], gr.at[i], exp=to_of(i))
 
     for i in range(1, n_exp):
         k = order(i, inner)
         send_g[k - 1] = jnp.dot(table(to_of(k)), scaled, preferred_element_type=F32).astype(BF16)
         g_copy(k).start()
-    g_all[me_z] = jnp.dot(table(me_z), scaled, preferred_element_type=F32).astype(BF16)
+    g_all[0] = jnp.dot(table(me_z), scaled, preferred_element_type=F32).astype(BF16)
 
     for i in range(1, n_exp):
         k = order(i, 1 - inner)
-        block = from_of(k)
-        remote(send_x.at[k - 1], x_all.at[me_d, block], xs.at[k - 1], xr.at[block], exp=block).wait_recv()
+        remote(send_x.at[k - 1], x_all.at[me_d, k], xs.at[k - 1], xr.at[k], exp=from_of(k)).wait_recv()
         for d in range(1, n_dp):
-            forward(d, block).start()
+            forward(d, k).start()
 
     in_win.wait()
     own_x = x_all[me_d].astype(F32).reshape(n_exp * cap, width).astype(BF16)
@@ -143,31 +142,39 @@
     dsilu[...] = (sigma * (1.0 + pre * (1.0 - sigma))).reshape(n_exp, cap, hidden)
     in_wout.wait()
 
-    def expert_block(block):
+    def g_wait(k):
+        remote(send_g.at[k - 1], g_all.at[k], gs.at[k - 1], gr.at[k], exp=from_of(k)).wait_recv()
+
+    def b_copy(k):
+        return remote(ret.at[k - 1], back.at[k], bs.at[k - 1], br.at[k], exp=from_of(k))
+
+    def expert_blocks(first, last):
+        count = last - first
+        rows = g_all[first:last].astype(F32).reshape(count * cap, width).astype(BF16)
         grad_h = lax.dot_general(
-            g_all[block], wout_v[...], (((1,), (1,)), ((), ())), preferred_element_type=F32
+            rows, wout_v[...], (((1,), (1,)), ((), ())), preferred_element_type=F32
         )
-        grad_pre = (grad_h * dsilu[block]).astype(BF16)
+        scale = dsilu[first:last].reshape(count * cap, hidden)
+        grad_pre = (grad_h * scale).astype(BF16)
+        grad_x = lax.dot_general(
+            grad_pre, win_v[...], (((1,), (1,)), ((), ())), preferred_element_type=F32
+        ).reshape(count, cap, width)
+        for k in range(first, last):
+            if k:
+                ret[k - 1] = grad_x[k - first].astype(BF16)
+                b_copy(k).start()
+            else:
+                back[0] = grad_x[0].astype(BF16)
+        wide = grad_pre.astype(F32).reshape(count, cap, hidden).astype(BF16)
         for j in range(n_dp):
-            gp_send[j, block] = grad_pre[:, j * part:(j + 1) * part]
-        return lax.dot_general(
-            grad_pre, win_v[...], (((1,), (1,)), ((), ())), preferred_element_type=F32
-        ).astype(BF16)
-
-    def b_copy(i, block):
-        return remote(ret.at[i - 1], back.at[me_z], bs.at[i - 1], br.at[me_z], exp=block)
-
-    back[me_z] = expert_block(me_z)
-
-    def one_block(i, carry):
-        k = order(i, 1 - inner)
-        block = from_of(k)
-        remote(send_g.at[k - 1], g_all.at[block], gs.at[k - 1], gr.at[block], exp=block).wait_recv()
-        ret[k - 1] = expert_block(block)
-        b_copy(k, block).start()
-        return carry
-
-    lax.fori_loop(1, n_exp, one_block, 0)
+            gp_send[j, first:last] = wide[:, :, j * part:(j + 1) * part]
+
+    for k in range(1, half):
+        g_wait(k)
+    expert_blocks(0, half)
+    for k in range(half, n_exp):
+        g_wait(k)
+    expert_blocks(half, n_exp)
 
     def p_copy(d):
         other = lax.rem(me_d + d, n_dp)
@@ -176,7 +183,7 @@
     for d in range(1, n_dp):
         p_copy(d).start()
     gp_all[me_d] = gp_send[me_d]
-    acc[...] = jnp.dot(table_t(me_z), back[me_z], preferred_element_type=F32)
+    acc[...] = jnp.dot(table_t(me_z), back[0], preferred_element_type=F32)
 
     for d in range(1, n_dp):
         other = lax.rem(me_d + n_dp - d, n_dp)
@@ -206,9 +213,8 @@
 
     for i in range(1, n_exp):
         k = order(i, inner)
-        block = to_of(k)
-        remote(ret.at[k - 1], back.at[block], bs.at[k - 1], br.at[block], exp=block).wait_recv()
-        total = acc[...] + jnp.dot(table_t(block), back[block], preferred_element_type=F32)
+        remote(ret.at[k - 1], back.at[k], bs.at[k - 1], br.at[k], exp=to_of(k)).wait_recv()
+        total = acc[...] + jnp.dot(table_t(to_of(k)), back[k], preferred_element_type=F32)
         if i < n_exp - 1:
             acc[...] = total
         else:
@@ -220,7 +226,7 @@
     for i in range(1, n_exp):
         x_copy(i).wait_send()
         g_copy(i).wait_send()
-        b_copy(i, from_of(i)).wait_send()
+        b_copy(i).wait_send()
     for d in range(1, n_dp):
         for block in range(n_exp):
             forward(d, block).wait_send()

time: 52.9 us -> 53 us (level)
  the two profiles are of different devices: /device:TPU:0 before, /device:TPU:15 now
where the time goes in v4:
time: 53 us; the launch traced here: 52.8 us
  Pallas kernels  52.2 us (98%)
  between operations  0.64 us (1%)
    pallas_call x1, Pallas kernels, body(): pl.pallas_call(functools.partial(kernel, (n_seg, n_dp, n_exp, cap, chunks...  49.7 us
    pallas_call x1, Pallas kernels, body(): pl.pallas_call(functools.partial(hand_on, pieces), out_shape=(jax.ShapeDt...  2.44 us

profile of v4, /device:TPU:15, one launch (start us, length us, event | category | flops | bytes accessed | tf_op | source)
XLA Modules:
  0.0 52.8 jit_solution(10350765164735095785)
XLA Ops:
  0.6 49.7 %shard_map.77 = (bf16[128,2048]{1,0:T(8,128)(2,1)}, bf16[2048,384]{1,0:T(8,128)(2,1)}) custom-call(s32[1,128]{1,0:T(1,128)} %bitcast.6, f32[1,128]{1,0:T(1,128)} %bitcast.7, bf16[1,128,2048]{2,1,0:T(8,128)(2,1)} %saved_hbm.1, bf16[1,128,2048]{2,1,0:T(8,128)(2,1)} %gy_hbm.1, bf16[1,1,2048,768]{3,2,1,0:T(8,128)(2,1)} %win_hbm.1, bf16[1,1,768,2048]{3,2,1,0:T(8,128)(2,1)} %wout_hbm.1), custom_call_target="tpu_custom_call" | custom-call | flops 2013265920 | bytes 10485760 | tf_op jit(solution)/shard_map/pallas_call | solution.py:268
  50.4 2.4 %shard_map.78 = (bf16[128,2048]{1,0:T(8,128)(2,1)}, bf16[2048,384]{1,0:T(8,128)(2,1)}) custom-call(bf16[128,2048]{1,0:T(8,128)(2,1)} %get-tuple-element.6.gx_ref, bf16[2048,384]{1,0:T(8,128)(2,1)} %get-tuple-element.7.gin_ref), custom_call_target="tpu_custom_call" | custom-call | tf_op jit(solution)/shard_map/pallas_call | solution.py:308

commit v5 on v4

--- a/solution.py
+++ b/solution.py
@@ -13,9 +13,9 @@
 def kernel(
     sizes,
     route_ref, gate_ref, saved_hbm, gy_hbm, win_hbm, wout_hbm,
-    gx_hbm, gin_hbm,
+    back, pick_hbm, gin_hbm,
     saved_v, cot, win_v, wout_v, send_x, send_g, x_all, g_all, dsilu,
-    gp_send, gp_all, ret, back, acc, gx_v, gin_v,
+    gp_send, gp_all, ret, own_ret, pick, gin_v,
     loc, seg_s, seg_r, xs, xr, gs, gr, fs, fr, ps, pr, bs, br, outs,
 ):
     n_seg, n_dp, n_exp, cap, chunks = sizes
@@ -87,23 +87,33 @@
         slots = lax.broadcasted_iota(jnp.int32, (cap, tok), 0) + expert * cap
         return (slots == pos_row).astype(F32).astype(BF16)
 
-    def table_t(expert):
-        slots = lax.broadcasted_iota(jnp.int32, (tok, cap), 1) + expert * cap
-        return (slots == pos_col).astype(F32).astype(BF16)
+    if paired:
+        apart, bit = route * 0, 1
+        while bit < n_exp:
+            one, two = route // bit % 2, me_z // bit % 2
+            apart = apart + bit * (one + two - 2 * one * two)
+            bit *= 2
+    else:
+        apart = lax.rem(route + n_exp - me_z, n_exp)
+    places = lax.broadcasted_iota(jnp.int32, (tok, n_exp * cap), 1)
+    pick[...] = (places == apart * cap + rank).astype(F32).astype(BF16)
+    out_pick = pltpu.make_async_copy(pick, pick_hbm, loc.at[4])
+    out_pick.start()
+
+    in_saved.wait()
+    saved = saved_v[...]
+    for i in range(1, n_exp):
+        send_x[i - 1] = jnp.dot(table(to_of(i)), saved, preferred_element_type=F32).astype(BF16)
 
     pl.semaphore_wait(barrier, len(peers))
     seg_copy = remote(gy_hbm.at[0], cot, seg_s.at[0], seg_r.at[0], seg=before_s)
     seg_copy.start()
-    in_saved.wait()
-    saved = saved_v[...]
 
     def x_copy(i):
         return remote(send_x.at[i - 1], x_all.at[me_d, i], xs.at[i - 1], xr.at[i], exp=to_of(i))
 
     for i in range(1, n_exp):
-        k = order(i, inner)
-        send_x[k - 1] = jnp.dot(table(to_of(k)), saved, preferred_element_type=F32).astype(BF16)
-        x_copy(k).start()
+        x_copy(order(i, inner)).start()
     in_win.start()
     in_wout.start()
     x_all[me_d, 0] = jnp.dot(table(me_z), saved, preferred_element_type=F32).astype(BF16)
@@ -124,9 +134,8 @@
         return remote(send_g.at[i - 1], g_all.at[i], gs.at[i - 1], gr.at[i], exp=to_of(i))
 
     for i in range(1, n_exp):
-        k = order(i, inner)
-        send_g[k - 1] = jnp.dot(table(to_of(k)), scaled, preferred_element_type=F32).astype(BF16)
-        g_copy(k).start()
+        send_g[i - 1] = jnp.dot(table(to_of(i)), scaled, preferred_element_type=F32).astype(BF16)
+        g_copy(i).start()
     g_all[0] = jnp.dot(table(me_z), scaled, preferred_element_type=F32).astype(BF16)
 
     for i in range(1, n_exp):
@@ -147,6 +156,8 @@
 
     def b_copy(k):
         return remote(ret.at[k - 1], back.at[k], bs.at[k - 1], br.at[k], exp=from_of(k))
+
+    own_back = pltpu.make_async_copy(own_ret, back.at[0], loc.at[3])
 
     def expert_blocks(first, last):
         count = last - first
@@ -164,7 +175,8 @@
                 ret[k - 1] = grad_x[k - first].astype(BF16)
                 b_copy(k).start()
             else:
-                back[0] = grad_x[0].astype(BF16)
+                own_ret[...] = grad_x[0].astype(BF16)
+                own_back.start()
         wide = grad_pre.astype(F32).reshape(count, cap, hidden).astype(BF16)
         for j in range(n_dp):
             gp_send[j, first:last] = wide[:, :, j * part:(j + 1) * part]
@@ -174,7 +186,7 @@
     expert_blocks(0, half)
     for k in range(half, n_exp):
         g_wait(k)
-    expert_blocks(half, n_exp)
+        expert_blocks(k, k + 1)
 
     def p_copy(d):
         other = lax.rem(me_d + d, n_dp)
@@ -183,7 +195,6 @@
     for d in range(1, n_dp):
         p_copy(d).start()
     gp_all[me_d] = gp_send[me_d]
-    acc[...] = jnp.dot(table_t(me_z), back[0], preferred_element_type=F32)
 
     for d in range(1, n_dp):
         other = lax.rem(me_d + n_dp - d, n_dp)
@@ -211,16 +222,8 @@
 
     lax.fori_loop(0, chunks, one_chunk, 0)
 
-    for i in range(1, n_exp):
-        k = order(i, inner)
+    for k in range(1, n_exp):
         remote(ret.at[k - 1], back.at[k], bs.at[k - 1], br.at[k], exp=to_of(k)).wait_recv()
-        total = acc[...] + jnp.dot(table_t(to_of(k)), back[k], preferred_element_type=F32)
-        if i < n_exp - 1:
-            acc[...] = total
-        else:
-            gx_v[...] = total.astype(BF16)
-    out_x = pltpu.make_async_copy(gx_v, gx_hbm, loc.at[3])
-    out_x.start()
 
     seg_copy.wait_send()
     for i in range(1, n_exp):
@@ -233,24 +236,36 @@
         p_copy(d).wait_send()
     for c in range(chunks):
         out_copy(c).wait()
-    out_x.wait()
-
-
-def hand_on(pieces, gx_ref, gin_ref, gx_out, gin_out, gx_v, gin_v, sems):
+    own_back.wait()
+    out_pick.wait()
+
+
+def hand_on(pieces, back_ref, pick_ref, gin_ref, gx_out, gin_out, back_v, pick_v, gin_v, gx_v, sems):
+    rows = gin_ref.shape[0] // pieces
+    count, cap, width = back_ref.shape
+    load_pick = pltpu.make_async_copy(pick_ref, pick_v, sems.at[2, 0])
+    load_back = pltpu.make_async_copy(back_ref, back_v, sems.at[2, 1])
+    store_x = pltpu.make_async_copy(gx_v, gx_out, sems.at[2, 2])
     loads, stores = [], []
-    for src, mid, dst in ((gin_ref, gin_v, gin_out), (gx_ref, gx_v, gx_out)):
-        rows = src.shape[0] // pieces
-        for p in range(pieces):
-            at = pl.ds(p * rows, rows)
-            loads.append(pltpu.make_async_copy(src.at[at], mid.at[at], sems.at[0, len(loads)]))
-            stores.append(pltpu.make_async_copy(mid.at[at], dst.at[at], sems.at[1, len(stores)]))
+    for p in range(pieces):
+        at = pl.ds(p * rows, rows)
+        loads.append(pltpu.make_async_copy(gin_ref.at[at], gin_v.at[at], sems.at[0, p]))
+        stores.append(pltpu.make_async_copy(gin_v.at[at], gin_out.at[at], sems.at[1, p]))
+    load_pick.start()
+    load_back.start()
     for load in loads:
         load.start()
+    load_pick.wait()
+    load_back.wait()
+    held = back_v[...].astype(F32).reshape(count * cap, width).astype(BF16)
+    gx_v[...] = jnp.dot(pick_v[...], held, preferred_element_type=F32).astype(BF16)
+    store_x.start()
     for load, store in zip(loads, stores):
         load.wait()
         store.start()
     for store in stores:
         store.wait()
+    store_x.wait()
 
 
 def body(saved_b, route_b, gate_b, grad_y_b, w_in, w_out):
@@ -265,14 +280,15 @@
     hbm = pl.BlockSpec(memory_space=pl.ANY)
     dma = pltpu.SemaphoreType.DMA
     flops = 8 * n_exp * cap * width * hidden
-    grad_x, grad_in = pl.pallas_call(
+    back, pick, grad_in = pl.pallas_call(
         functools.partial(kernel, (n_seg, n_dp, n_exp, cap, chunks)),
         out_shape=(
-            jax.ShapeDtypeStruct((tok, width), BF16),
+            jax.ShapeDtypeStruct((n_exp, cap, width), BF16),
+            jax.ShapeDtypeStruct((tok, n_exp * cap), BF16),
             jax.ShapeDtypeStruct((width, part), BF16),
         ),
         in_specs=[vmem, vmem, hbm, hbm, hbm, hbm],
-        out_specs=(hbm, hbm),
+        out_specs=(hbm, hbm, hbm),
         scratch_shapes=[
             pltpu.VMEM((tok, width), BF16),
             pltpu.VMEM((tok, width), BF16),
@@ -286,11 +302,10 @@
             pltpu.VMEM((n_dp, n_exp, cap, part), BF16),
             pltpu.VMEM((n_dp, n_exp, cap, part), BF16),
             pltpu.VMEM((n_exp - 1, cap, width), BF16),
-            pltpu.VMEM((n_exp, cap, width), BF16),
-            pltpu.VMEM((tok, width), F32),
-            pltpu.VMEM((tok, width), BF16),
+            pltpu.VMEM((cap, width), BF16),
+            pltpu.VMEM((tok, n_exp * cap), BF16),
             pltpu.VMEM((width, part), BF16),
-            dma((4,)),
+            dma((5,)),
             dma((1,)), dma((1,)),
             dma((n_exp,)), dma((n_exp,)),
             dma((n_exp,)), dma((n_exp,)),
@@ -311,13 +326,17 @@
             jax.ShapeDtypeStruct((tok, width), BF16),
             jax.ShapeDtypeStruct((width, part), BF16),
         ),
-        in_specs=[hbm, hbm],
+        in_specs=[hbm, hbm, hbm],
         out_specs=(hbm, hbm),
         scratch_shapes=[
-            pltpu.VMEM((tok, width), BF16), pltpu.VMEM((width, part), BF16), dma((2, 2 * pieces)),
+            pltpu.VMEM((n_exp, cap, width), BF16),
+            pltpu.VMEM((tok, n_exp * cap), BF16),
+            pltpu.VMEM((width, part), BF16),
+            pltpu.VMEM((tok, width), BF16),
+            dma((3, pieces)),
         ],
         compiler_params=pltpu.CompilerParams(vmem_limit_bytes=56 * 1024 * 1024),
-    )(grad_x, grad_in)
+    )(back, pick, grad_in)
     return (grad_x[None], grad_in[None, None])
 
 

time: 53 us -> 53.9 us (1.017)
  the two profiles are of different devices: /device:TPU:15 before, /device:TPU:20 now
where the time goes in v5:
time: 53.9 us; the launch traced here: 53.7 us
  Pallas kernels  53 us (98%)
  between operations  0.64 us (1%)
    pallas_call x1, Pallas kernels, body(): pl.pallas_call(functools.partial(kernel, (n_seg, n_dp, n_exp, cap, chunks...  50.2 us
    pallas_call x1, Pallas kernels, body(): pl.pallas_call(functools.partial(hand_on, pieces), out_shape=(jax.ShapeDt...  2.83 us

profile of v5, /device:TPU:20, one launch (start us, length us, event | category | flops | bytes accessed | tf_op | source)
XLA Modules:
  0.0 53.7 jit_solution(17936219302622820685)
XLA Ops:
  0.6 50.2 %shard_map.77 = (bf16[4,40,2048]{2,1,0:T(8,128)(2,1)}, bf16[128,160]{1,0:T(8,128)(2,1)}, bf16[2048,384]{1,0:T(8,128)(2,1)}) custom-call(s32[1,128]{1,0:T(1,128)} %bitcast.6, f32[1,128]{1,0:T(1,128)} %bitcast.7, bf16[1,128,2048]{2,1,0:T(8,128)(2,1)} %saved_hbm.1, bf16[1,128,2048]{2,1,0:T(8,128)(2,1)} %gy_hbm.1, bf16[1,1,2048,768]{3,2,1,0:T(8,128)(2,1)} %win_hbm.1, ...), custom_call_target="tpu_custom_call" | custom-call | flops 2013265920 | bytes 10485760 | tf_op jit(solution)/shard_map/pallas_call | solution.py:283
  50.8 2.8 %shard_map.78 = (bf16[128,2048]{1,0:T(8,128)(2,1)}, bf16[2048,384]{1,0:T(8,128)(2,1)}) custom-call(bf16[4,40,2048]{2,1,0:T(8,128)(2,1)} %get-tuple-element.7.back_ref, bf16[128,160]{1,0:T(8,128)(2,1)} %get-tuple-element.8.pick_ref, bf16[2048,384]{1,0:T(8,128)(2,1)} %get-tuple-element.9.gin_ref), custom_call_target="tpu_custom_call" | custom-call | tf_op jit(solution)/shard_map/pallas_call | solution.py:323

commit v6 on v5

--- a/solution.py
+++ b/solution.py
@@ -107,12 +107,13 @@
 
     pl.semaphore_wait(barrier, len(peers))
     seg_copy = remote(gy_hbm.at[0], cot, seg_s.at[0], seg_r.at[0], seg=before_s)
-    seg_copy.start()
 
     def x_copy(i):
         return remote(send_x.at[i - 1], x_all.at[me_d, i], xs.at[i - 1], xr.at[i], exp=to_of(i))
 
-    for i in range(1, n_exp):
+    x_copy(order(1, inner)).start()
+    seg_copy.start()
+    for i in range(2, n_exp):
         x_copy(order(i, inner)).start()
     in_win.start()
     in_wout.start()

time: 53.9 us -> 53.9 us (level)
  no operation moved by 1% of the time
where the time goes in v6:
time: 53.9 us; the launch traced here: 53.7 us
  Pallas kernels  53 us (98%)
  between operations  0.64 us (1%)
    pallas_call x1, Pallas kernels, body(): pl.pallas_call(functools.partial(kernel, (n_seg, n_dp, n_exp, cap, chunks...  50.2 us
    pallas_call x1, Pallas kernels, body(): pl.pallas_call(functools.partial(hand_on, pieces), out_shape=(jax.ShapeDt...  2.83 us

profile of v6, /device:TPU:20, one launch (start us, length us, event | category | flops | bytes accessed | tf_op | source)
XLA Modules:
  0.0 53.7 jit_solution(42537584986418890)
XLA Ops:
  0.6 50.2 %shard_map.77 = (bf16[4,40,2048]{2,1,0:T(8,128)(2,1)}, bf16[128,160]{1,0:T(8,128)(2,1)}, bf16[2048,384]{1,0:T(8,128)(2,1)}) custom-call(s32[1,128]{1,0:T(1,128)} %bitcast.6, f32[1,128]{1,0:T(1,128)} %bitcast.7, bf16[1,128,2048]{2,1,0:T(8,128)(2,1)} %saved_hbm.1, bf16[1,128,2048]{2,1,0:T(8,128)(2,1)} %gy_hbm.1, bf16[1,1,2048,768]{3,2,1,0:T(8,128)(2,1)} %win_hbm.1, ...), custom_call_target="tpu_custom_call" | custom-call | flops 2013265920 | bytes 10485760 | tf_op jit(solution)/shard_map/pallas_call | solution.py:284
  50.8 2.8 %shard_map.78 = (bf16[128,2048]{1,0:T(8,128)(2,1)}, bf16[2048,384]{1,0:T(8,128)(2,1)}) custom-call(bf16[4,40,2048]{2,1,0:T(8,128)(2,1)} %get-tuple-element.7.back_ref, bf16[128,160]{1,0:T(8,128)(2,1)} %get-tuple-element.8.pick_ref, bf16[2048,384]{1,0:T(8,128)(2,1)} %get-tuple-element.9.gin_ref), custom_call_target="tpu_custom_call" | custom-call | tf_op jit(solution)/shard_map/pallas_call | solution.py:324

commit v7 on v6

--- a/solution.py
+++ b/solution.py
@@ -43,8 +43,14 @@
     half = max(1, n_exp // 2)
     inner = (me_z + half // 2) // half % 2
 
-    def order(i, far_first):
-        return 1 + lax.rem(i - 1 + far_first * (half - 1), max(1, n_exp - 1))
+    near, far = list(range(1, half)), list(range(half, n_exp))
+
+    def by_place(ends, inners):
+        return [end + inner * (mid - end) for end, mid in zip(ends, inners)]
+
+    order_x = by_place(near + far, far[::-1] + near)
+    order_far = by_place(far, far[::-1])
+    order_g = near + order_far
 
     def remote(src, dst, ss, rs, seg=None, dp=None, exp=None):
         dev = (
@@ -111,10 +117,9 @@
     def x_copy(i):
         return remote(send_x.at[i - 1], x_all.at[me_d, i], xs.at[i - 1], xr.at[i], exp=to_of(i))
 
-    x_copy(order(1, inner)).start()
     seg_copy.start()
-    for i in range(2, n_exp):
-        x_copy(order(i, inner)).start()
+    for k in order_x:
+        x_copy(k).start()
     in_win.start()
     in_wout.start()
     x_all[me_d, 0] = jnp.dot(table(me_z), saved, preferred_element_type=F32).astype(BF16)
@@ -134,13 +139,12 @@
     def g_copy(i):
         return remote(send_g.at[i - 1], g_all.at[i], gs.at[i - 1], gr.at[i], exp=to_of(i))
 
-    for i in range(1, n_exp):
-        send_g[i - 1] = jnp.dot(table(to_of(i)), scaled, preferred_element_type=F32).astype(BF16)
-        g_copy(i).start()
+    for k in order_g:
+        send_g[k - 1] = jnp.dot(table(to_of(k)), scaled, preferred_element_type=F32).astype(BF16)
+        g_copy(k).start()
     g_all[0] = jnp.dot(table(me_z), scaled, preferred_element_type=F32).astype(BF16)
 
-    for i in range(1, n_exp):
-        k = order(i, 1 - inner)
+    for k in order_g:
         remote(send_x.at[k - 1], x_all.at[me_d, k], xs.at[k - 1], xr.at[k], exp=from_of(k)).wait_recv()
         for d in range(1, n_dp):
             forward(d, k).start()
@@ -160,34 +164,41 @@
 
     own_back = pltpu.make_async_copy(own_ret, back.at[0], loc.at[3])
 
-    def expert_blocks(first, last):
-        count = last - first
-        rows = g_all[first:last].astype(F32).reshape(count * cap, width).astype(BF16)
+    def expert_rows(rows, scale):
         grad_h = lax.dot_general(
             rows, wout_v[...], (((1,), (1,)), ((), ())), preferred_element_type=F32
         )
-        scale = dsilu[first:last].reshape(count * cap, hidden)
         grad_pre = (grad_h * scale).astype(BF16)
-        grad_x = lax.dot_general(
+        return grad_pre, lax.dot_general(
             grad_pre, win_v[...], (((1,), (1,)), ((), ())), preferred_element_type=F32
-        ).reshape(count, cap, width)
-        for k in range(first, last):
-            if k:
-                ret[k - 1] = grad_x[k - first].astype(BF16)
-                b_copy(k).start()
-            else:
-                own_ret[...] = grad_x[0].astype(BF16)
-                own_back.start()
-        wide = grad_pre.astype(F32).reshape(count, cap, hidden).astype(BF16)
+        )
+
+    def near_blocks():
+        rows = g_all[:half].astype(F32).reshape(half * cap, width).astype(BF16)
+        grad_pre, grad_x = expert_rows(rows, dsilu[:half].reshape(half * cap, hidden))
+        grad_x = grad_x.reshape(half, cap, width)
+        for k in near:
+            ret[k - 1] = grad_x[k].astype(BF16)
+            b_copy(k).start()
+        own_ret[...] = grad_x[0].astype(BF16)
+        own_back.start()
+        wide = grad_pre.astype(F32).reshape(half, cap, hidden).astype(BF16)
         for j in range(n_dp):
-            gp_send[j, first:last] = wide[:, :, j * part:(j + 1) * part]
+            gp_send[j, :half] = wide[:, :, j * part:(j + 1) * part]
+
+    def far_block(k):
+        grad_pre, grad_x = expert_rows(g_all[k], dsilu[k])
+        ret[k - 1] = grad_x.astype(BF16)
+        b_copy(k).start()
+        for j in range(n_dp):
+            gp_send[j, k] = grad_pre[:, j * part:(j + 1) * part]
 
     for k in range(1, half):
         g_wait(k)
-    expert_blocks(0, half)
-    for k in range(half, n_exp):
+    near_blocks()
+    for k in order_far:
         g_wait(k)
-        expert_blocks(k, k + 1)
+        far_block(k)
 
     def p_copy(d):
         other = lax.rem(me_d + d, n_dp)

time: 53.9 us -> 53.7 us (level)
  the two profiles are of different devices: /device:TPU:20 before, /device:TPU:0 now
where the time goes in v7:
time: 53.7 us; the launch traced here: 53.5 us
  Pallas kernels  52.9 us (99%)
  between operations  0.64 us (1%)
    pallas_call x1, Pallas kernels, body(): pl.pallas_call(functools.partial(kernel, (n_seg, n_dp, n_exp, cap, chunks...  50.1 us
    pallas_call x1, Pallas kernels, body(): pl.pallas_call(functools.partial(hand_on, pieces), out_shape=(jax.ShapeDt...  2.84 us

profile of v7, /device:TPU:0, one launch (start us, length us, event | category | flops | bytes accessed | tf_op | source)
XLA Modules:
  0.0 53.5 jit_solution(6276829857751785772)
XLA Ops:
  0.6 50.1 %shard_map.77 = (bf16[4,40,2048]{2,1,0:T(8,128)(2,1)}, bf16[128,160]{1,0:T(8,128)(2,1)}, bf16[2048,384]{1,0:T(8,128)(2,1)}) custom-call(s32[1,128]{1,0:T(1,128)} %bitcast.6, f32[1,128]{1,0:T(1,128)} %bitcast.7, bf16[1,128,2048]{2,1,0:T(8,128)(2,1)} %saved_hbm.1, bf16[1,128,2048]{2,1,0:T(8,128)(2,1)} %gy_hbm.1, bf16[1,1,2048,768]{3,2,1,0:T(8,128)(2,1)} %win_hbm.1, ...), custom_call_target="tpu_custom_call" | custom-call | flops 2013265920 | bytes 10485760 | tf_op jit(solution)/shard_map/pallas_call | solution.py:295
  50.7 2.8 %shard_map.78 = (bf16[128,2048]{1,0:T(8,128)(2,1)}, bf16[2048,384]{1,0:T(8,128)(2,1)}) custom-call(bf16[4,40,2048]{2,1,0:T(8,128)(2,1)} %get-tuple-element.7.back_ref, bf16[128,160]{1,0:T(8,128)(2,1)} %get-tuple-element.8.pick_ref, bf16[2048,384]{1,0:T(8,128)(2,1)} %get-tuple-element.9.gin_ref), custom_call_target="tpu_custom_call" | custom-call | tf_op jit(solution)/shard_map/pallas_call | solution.py:335

commit v8 on v7

--- a/solution.py
+++ b/solution.py
@@ -45,11 +45,13 @@
 
     near, far = list(range(1, half)), list(range(half, n_exp))
 
-    def by_place(ends, inners):
-        return [end + inner * (mid - end) for end, mid in zip(ends, inners)]
-
-    order_x = by_place(near + far, far[::-1] + near)
-    order_far = by_place(far, far[::-1])
+    lower = inner * (1 - me_z // half)
+    turned = [lower * (b - a) for a, b in zip(far, far[::-1])]
+    order_far = [k + t for k, t in zip(far, turned)]
+    order_x = [
+        end + inner * (mid - end) + t
+        for end, mid, t in zip(near + far, far + near, turned + [0] * len(near))
+    ]
     order_g = near + order_far
 
     def remote(src, dst, ss, rs, seg=None, dp=None, exp=None):

time: 53.7 us -> 51.8 us (0.965)
  the two profiles are of different devices: /device:TPU:0 before, /device:TPU:25 now
where the time goes in v8:
time: 51.8 us; the launch traced here: 51.6 us
  Pallas kernels  51 us (98%)
  between operations  0.64 us (1%)
    pallas_call x1, Pallas kernels, body(): pl.pallas_call(functools.partial(kernel, (n_seg, n_dp, n_exp, cap, chunks...  48.2 us
    pallas_call x1, Pallas kernels, body(): pl.pallas_call(functools.partial(hand_on, pieces), out_shape=(jax.ShapeDt...  2.83 us

profile of v8, /device:TPU:25, one launch (start us, length us, event | category | flops | bytes accessed | tf_op | source)
XLA Modules:
  0.0 51.6 jit_solution(17726343171477066747)
XLA Ops:
  0.6 48.2 %shard_map.77 = (bf16[4,40,2048]{2,1,0:T(8,128)(2,1)}, bf16[128,160]{1,0:T(8,128)(2,1)}, bf16[2048,384]{1,0:T(8,128)(2,1)}) custom-call(s32[1,128]{1,0:T(1,128)} %bitcast.6, f32[1,128]{1,0:T(1,128)} %bitcast.7, bf16[1,128,2048]{2,1,0:T(8,128)(2,1)} %saved_hbm.1, bf16[1,128,2048]{2,1,0:T(8,128)(2,1)} %gy_hbm.1, bf16[1,1,2048,768]{3,2,1,0:T(8,128)(2,1)} %win_hbm.1, ...), custom_call_target="tpu_custom_call" | custom-call | flops 2013265920 | bytes 10485760 | tf_op jit(solution)/shard_map/pallas_call | solution.py:297
  48.8 2.8 %shard_map.78 = (bf16[128,2048]{1,0:T(8,128)(2,1)}, bf16[2048,384]{1,0:T(8,128)(2,1)}) custom-call(bf16[4,40,2048]{2,1,0:T(8,128)(2,1)} %get-tuple-element.7.back_ref, bf16[128,160]{1,0:T(8,128)(2,1)} %get-tuple-element.8.pick_ref, bf16[2048,384]{1,0:T(8,128)(2,1)} %get-tuple-element.9.gin_ref), custom_call_target="tpu_custom_call" | custom-call | tf_op jit(solution)/shard_map/pallas_call | solution.py:337
